TPU v7x, 256 devices: a whole 4x4x8 slice. The times are simulated.
256 devices in a mesh: atm: 32 (over y, z_lo, core), ocn: 4 (over x), ch: 2 (over z_hi).
Axes of the slice: x: 4, y: 4, z: 8 (z_hi: 2, z_lo: 4; z = z_hi * 4 + z_lo), core: 2. Of those that a mesh axis runs over, the one named last changes fastest.
Arguments:
- atmosphere: bfloat16 [384, 1440, 384], P('atm', ('ocn', 'ch')), may hold values from -6 to 6
- ocean_state: bfloat16 [384, 1440, 200], P('atm', ('ocn', 'ch')), may hold values from -6 to 6
- surface_flux: float32 [4, 384, 1440], P(None, 'atm', ('ocn', 'ch')), may hold values from -6 to 6
- land_sea: int32 [384, 1440], P('atm', ('ocn', 'ch')), may hold values 0 or 1
- surface_read: bfloat16 [200], replicated, may hold values from -0.4375 to 0.4375
- surface_gain: float32 [384], replicated, may hold values from -4 to 4
- legendre: bfloat16 [384, 384, 384], P('atm'), may hold values from -0.3125 to 0.3125
- spectral_gain: float32 [384, 384], P(None, ('ocn', 'ch')), may hold values from -4 to 4
- mixing: bfloat16 [384, 384], replicated, may hold values from -0.3125 to 0.3125
- flux_weight: bfloat16 [384, 4], replicated, may hold values from -0.3125 to 0.3125
- flux_embed: float32 [4, 200], replicated, may hold values from -3 to 3
- conv_kernel: float32 [7, 7, 200], replicated, may hold values from -0.875 to 0.875
- norm_gain: float32 [200], replicated, may hold values from 0.25 to 1.75
- ocean_up: bfloat16 [200, 800], replicated, may hold values from -0.4375 to 0.4375
- ocean_down: bfloat16 [800, 200], replicated, may hold values from -0.21875 to 0.21875
Outputs:
- atmosphere_next: bfloat16 [384, 1440, 384], P('atm', ('ocn', 'ch'))
- flux_next: float32 [4, 384, 1440], P(None, 'atm', ('ocn', 'ch'))
- ocean_next: bfloat16 [384, 1440, 200], P('atm', ('ocn', 'ch'))
All inputs are finite; a program needn't handle non-finite values. No bound on the sum of `land_sea` on one device may be relied on, other than what follows from the above.
Results may differ from a plain program's by a relative error of at most 0.009.
Values may be sent and summed in bfloat16 or wider, within the bound.
A program may use at most 128 MiB of HBM per device.

v0:
```python
import math

import jax
import jax.numpy as jnp
import ml_dtypes
import numpy as np
from jax import lax
from jax.experimental import pallas as pl
from jax.experimental.pallas import tpu as pltpu
from jax.sharding import PartitionSpec as P

M = 384
NLON = 1440
C = 384
OC = 200
HID = 800
LATS = 12
LONS = 180
ROWS = 192
CB = 48
PEERS = 32
MODES = 24
CHUNKS = ((0, 8, 384), (8, 4, 256))
MESH = pl.DeviceIdType.MESH
F32 = jnp.float32
BF16 = jnp.bfloat16
VMEM_LIMIT = 60 * 2**20


def lon_tables():
    lon = np.arange(NLON, dtype=np.int64)
    wave = np.arange(M, dtype=np.int64)
    phase = (lon[:, None] * wave[None, :]) % NLON
    angle = phase.astype(np.float32) * np.float32(2.0 * math.pi / NLON)
    table = np.stack([np.cos(angle), -np.sin(angle)], axis=2) * np.float32(NLON**-0.5)
    table = table.astype(np.float32).reshape(4, 2, LONS, 2 * M).transpose(1, 0, 2, 3)
    padded = np.zeros((2, 4, ROWS, 2 * M), np.float32)
    padded[:, :, :LONS] = table
    inverse = padded.reshape(2, 4 * ROWS, 2 * M).astype(ml_dtypes.bfloat16)
    return np.ascontiguousarray(inverse.transpose(0, 2, 1)), inverse


def segments(src, dst, count):
    out = []
    done = 0
    while done < count:
        s, d = src + done, dst + done
        step = min(count - done, 128 - s % 128, 128 - d % 128)
        out.append((s // 128, d // 128, (d - s) % 128, d % 128, d % 128 + step))
        done += step
    return out


def move_lanes(moves, tiles, get, rows):
    lane = lax.broadcasted_iota(jnp.int32, (rows, 128), 1)
    out = [None] * tiles
    for key, src, dst, count in moves:
        for s_tile, d_tile, shift, low, high in segments(src, dst, count):
            piece = get(key, s_tile)
            if shift:
                piece = pltpu.roll(piece, shift, axis=1)
            if out[d_tile] is None:
                if low == 0:
                    out[d_tile] = jnp.where(lane < high, piece, 0.0)
                else:
                    out[d_tile] = jnp.where((lane >= low) & (lane < high), piece, 0.0)
            else:
                out[d_tile] = jnp.where((lane >= low) & (lane < high), piece, out[d_tile])
    return out


def body(
    atm_ref, oc_ref, flux_ref, land_ref, read_ref, gain_ref, leg_hbm, sgain_ref, mix_ref, fw_ref,
    embed_ref, ck_ref, ngain_ref, up_ref, down_ref, tf_hbm, ti_hbm,
    atm_out, flux_out, oc_out,
    tf, ti, leg, leg_p, leg_t, forced,
    pack_a, pack_b, got_a, got_b, spec_a, spec_b, rspec_a, rspec_b, rsum, ssum,
    syn_a, syn_b, rsyn_a, rsyn_b, sy_a, sy_b, gs_a, gs_b, rg_a, rg_b,
    sg2, cols, colt, fws, drv, edge_l, edge_r, halo_l, halo_r, cpad, cker,
    in_sem, x_send, x_recv, z_send, z_recv, zi_send, zi_recv, xi_send, xi_recv, h_send, h_recv, loc_sem,
):
    pack, got, spec, rspec = (pack_a, pack_b), (got_a, got_b), (spec_a, spec_b), (rspec_a, rspec_b)
    syn, rsyn, sy, gs, rg = (syn_a, syn_b), (rsyn_a, rsyn_b), (sy_a, sy_b), (gs_a, gs_b), (rg_a, rg_b)
    a_id = lax.axis_index("atm")
    x = lax.axis_index("ocn")
    h = lax.axis_index("ch")
    core = lax.rem(a_id, 2)
    yz = a_id // 2
    y0 = yz // 4
    z0 = lax.rem(yz, 4)
    me = 2 * x + core
    lon_block = 2 * x + h
    self_peer = core == h
    n_remote = PEERS - self_peer.astype(jnp.int32)

    tf_copy = pltpu.make_async_copy(tf_hbm.at[h], tf, in_sem.at[0])
    ti_copy = pltpu.make_async_copy(ti_hbm.at[h], ti, in_sem.at[1])
    leg_copy = pltpu.make_async_copy(leg_hbm, leg, in_sem.at[2])
    tf_copy.start()
    leg_copy.start()
    ti_copy.start()

    def row_dev(q):
        return {"atm": 2 * yz + lax.rem(q, 2), "ocn": q // 2, "ch": h}

    def mode_dev(j):
        return {"atm": j, "ocn": x, "ch": core}

    def band_dev(j):
        return {"atm": (j // 2) * 2 + h, "ocn": x, "ch": lax.rem(j, 2)}

    def lat_dev(step):
        return {"atm": lax.rem(a_id + step + 32, 32), "ocn": x, "ch": h}

    def lon_dev(step):
        b = lax.rem(lon_block + step + 8, 8)
        return {"atm": a_id, "ocn": b // 2, "ch": lax.rem(b, 2)}

    barrier = pltpu.get_barrier_semaphore()

    def greet(device):
        pl.semaphore_signal(barrier, inc=1, device_id=device, device_id_type=MESH)

    def greet_row(i, carry):
        greet(row_dev(lax.rem(me + i, 8)))
        return carry

    lax.fori_loop(1, 8, greet_row, 0)
    for step in (-1, 1):
        greet(lat_dev(step))
        greet(lon_dev(step))

    def greet_peers(j, carry):
        @pl.when(jnp.logical_not(self_peer & (j == a_id)))
        def _():
            greet(mode_dev(j))

        @pl.when(jnp.logical_not(self_peer & (j == 2 * yz + h)))
        def _():
            greet(band_dev(j))

        return carry

    lax.fori_loop(0, PEERS, greet_peers, 0)

    forced[:, 176:192, :] = jnp.zeros((LATS, 16, C), BF16)

    def force(a, carry):
        seen = oc_ref[a].astype(F32) * read_ref[...].astype(F32)
        surface = jnp.sum(seen, axis=1, keepdims=True)
        forced[a, 0:LONS, :] = (atm_ref[a].astype(F32) + surface * gain_ref[...]).astype(BF16)
        return carry

    lax.fori_loop(0, LATS, force, 0)

    def pack_chunk(k):
        a0, na, width = CHUNKS[k]

        def rows_step(rb, carry):
            r0 = pl.multiple_of(rb * 48, 16)
            held = {}
            for a in range(na):
                for t in range(3):
                    held[a, t] = forced[a0 + a, pl.ds(r0, 48), 128 * t : 128 * t + 128].astype(F32)
            for q in range(8):
                moves = [(a, CB * q, CB * a, CB) for a in range(na)]
                tiles = move_lanes(moves, width // 128, lambda key, t: held[key, t], 48)
                for t, value in enumerate(tiles):
                    pack[k][q, pl.ds(r0, 48), 128 * t : 128 * t + 128] = value.astype(BF16)
            return carry

        lax.fori_loop(0, 4, rows_step, 0)

    def x_copy(k, q):
        return pltpu.make_async_remote_copy(
            src_ref=pack[k].at[q], dst_ref=got[k].at[core, x], send_sem=x_send.at[k],
            recv_sem=x_recv.at[k], device_id=row_dev(q), device_id_type=MESH,
        )

    def x_start(k):
        pltpu.make_async_copy(pack[k].at[me], got[k].at[core, x], loc_sem.at[k]).start()

        def go(i, carry):
            x_copy(k, lax.rem(me + i, 8)).start()
            return carry

        lax.fori_loop(1, 8, go, 0)

    def covers(ref, send, recv):
        return pltpu.make_async_remote_copy(
            src_ref=ref, dst_ref=ref, send_sem=send, recv_sem=recv,
            device_id=lat_dev(1), device_id_type=MESH,
        )

    def x_all(k, send, recv):
        return covers(pack[k].at[pl.ds(0, 7)], send.at[k], recv.at[k])

    def x_wait(k):
        pltpu.make_async_copy(pack[k].at[me], got[k].at[core, x], loc_sem.at[k]).wait()
        x_all(k, x_send, x_recv).wait_recv()

    pack_chunk(1)
    pl.semaphore_wait(barrier, 2 * n_remote + 7 + 4)
    x_start(1)
    pack_chunk(0)
    x_start(0)

    cols[...] = jnp.zeros_like(cols)
    for f in range(4):
        cols[16 * f : 16 * f + LATS, 0:LONS] = flux_ref[f]
    cols[64 : 64 + LATS, 0:LONS] = land_ref[...].astype(F32)
    colt[...] = jnp.transpose(cols[...], (1, 0))
    drv[3:15, 176:192, :] = jnp.zeros((LATS, 16, 256), BF16)
    drv[3:15, :, 128:256] = jnp.zeros((LATS, ROWS, 128), BF16)
    for a in range(LATS):
        total = oc_ref[a].astype(F32)
        for f in range(4):
            total = total + colt[0:LONS, 16 * f + a : 16 * f + a + 1] * embed_ref[f : f + 1, :]
        drv[a + 3, 0:LONS, 0:OC] = total.astype(BF16)

    lat_low = pltpu.make_async_remote_copy(
        src_ref=drv.at[pl.ds(12, 3)], dst_ref=drv.at[pl.ds(0, 3)], send_sem=h_send.at[0],
        recv_sem=h_recv.at[0], device_id=lat_dev(1), device_id_type=MESH,
    )
    lat_high = pltpu.make_async_remote_copy(
        src_ref=drv.at[pl.ds(3, 3)], dst_ref=drv.at[pl.ds(15, 3)], send_sem=h_send.at[1],
        recv_sem=h_recv.at[1], device_id=lat_dev(-1), device_id_type=MESH,
    )
    lat_low.start()
    lat_high.start()

    sg2[...] = jnp.zeros_like(sg2)
    sg2[:, 0:CB] = sgain_ref[...]
    sg2[...] = sg2[...] + pltpu.roll(sg2[...], CB, axis=1)
    fws[...] = jnp.zeros_like(fws)
    fws[:, 0:4] = fw_ref[...].astype(F32)
    fwt = jnp.transpose(fws[...], (1, 0))[0:16].astype(BF16)
    cker[...] = jnp.zeros_like(cker)
    for i in range(7):
        cker[8 * i : 8 * i + 7, 0:OC] = ck_ref[i]

    leg_copy.wait()
    new = lax.broadcasted_iota(jnp.int32, (C, C), 0)
    old = lax.broadcasted_iota(jnp.int32, (C, C), 1)
    order = (old == lax.rem(new, 32) * LATS + new // 32).astype(F32).astype(BF16)

    def permute(m, carry):
        table = leg[m]
        leg_p[m] = lax.dot_general(
            table, order, (((1,), (1,)), ((), ())), preferred_element_type=F32
        ).astype(BF16)
        leg_t[m] = lax.dot_general(
            order, table, (((1,), (1,)), ((), ())), preferred_element_type=F32
        ).astype(BF16)
        return carry

    lax.fori_loop(0, LATS, permute, 0)

    slot = 2 * yz + h

    def z_copy(k, j):
        return pltpu.make_async_remote_copy(
            src_ref=spec[k].at[j], dst_ref=rspec[k].at[slot], send_sem=z_send.at[k],
            recv_sem=z_recv.at[k], device_id=mode_dev(j), device_id_type=MESH,
        )

    def z_local(k):
        return pltpu.make_async_copy(spec[k].at[a_id], rspec[k].at[slot], loc_sem.at[2 + k])

    def forward(k):
        width = CHUNKS[k][2]

        def step(i, carry):
            yb = lax.rem(y0 + i, 4)
            lhs = tf[pl.ds(pl.multiple_of(yb * 192, 16), 192), :]
            halves = [
                jnp.dot(lhs, got[k][s].reshape(4 * ROWS, width), preferred_element_type=F32)
                for s in range(2)
            ]
            for n in range(8):
                part = slice(MODES * n, MODES * n + MODES)
                both = jnp.concatenate([halves[0][part], halves[1][part]], axis=0)
                spec[k][yb * 8 + n] = both.astype(BF16)

            def send(n, c2):
                j = yb * 8 + lax.rem(2 * z0 + n, 8)
                mine = self_peer & (j == a_id)

                @pl.when(jnp.logical_not(mine))
                def _():
                    z_copy(k, j).start()

                @pl.when(mine)
                def _():
                    z_local(k).start()

                return c2

            lax.fori_loop(0, 8, send, 0)
            return carry

        lax.fori_loop(0, 4, step, 0)

    def peers_all(k, send, recv, act):
        @pl.when(self_peer)
        def _():
            act(covers(rspec[k].at[pl.ds(0, PEERS - 1)], send.at[k], recv.at[k]))

        @pl.when(jnp.logical_not(self_peer))
        def _():
            act(covers(rspec[k], send.at[k], recv.at[k]))

    tf_copy.wait()
    x_wait(1)
    forward(1)

    lat_low.wait_recv()
    lat_high.wait_recv()

    @pl.when(a_id == 0)
    def _():
        drv[0:3] = jnp.zeros((3, ROWS, 256), BF16)

    @pl.when(a_id == 31)
    def _():
        drv[15:18] = jnp.zeros((3, ROWS, 256), BF16)

    edge_l[...] = drv[:, 0:16, :]
    edge_r[...] = drv[:, 176:192, :]
    lon_low = pltpu.make_async_remote_copy(
        src_ref=edge_r, dst_ref=halo_l, send_sem=h_send.at[2],
        recv_sem=h_recv.at[2], device_id=lon_dev(1), device_id_type=MESH,
    )
    lon_high = pltpu.make_async_remote_copy(
        src_ref=edge_l, dst_ref=halo_r, send_sem=h_send.at[3],
        recv_sem=h_recv.at[3], device_id=lon_dev(-1), device_id_type=MESH,
    )
    lon_low.start()
    lon_high.start()

    x_wait(0)
    forward(0)

    lon_low.wait_recv()
    lon_high.wait_recv()

    def place(r, carry):
        cpad[r, 0:8, :] = pltpu.roll(halo_l[r].astype(F32), 15, axis=0)[0:8]
        cpad[r, 176:192, :] = jnp.zeros((16, 256), F32)
        cpad[r, 183:189, :] = halo_r[r].astype(F32)[0:6]
        cpad[r, 3:183, :] = drv[r, 0:LONS, :].astype(F32)
        return carry

    lax.fori_loop(0, LATS + 6, place, 0)
    lane = lax.broadcasted_iota(jnp.int32, (ROWS, 256), 1)

    def ocean(a, carry):
        halves = []
        for t in range(2):
            part = slice(128 * t, 128 * t + 128)
            total = None
            for j in range(7):
                acc = None
                for i in range(7):
                    term = cker[8 * i + j : 8 * i + j + 1, part] * cpad[a + i, :, part]
                    acc = term if acc is None else acc + term
                if j:
                    acc = pltpu.roll(acc, ROWS - j, axis=0)
                total = acc if total is None else total + acc
            halves.append(total)
        conv = jnp.concatenate(halves, axis=1)
        mean = jnp.sum(conv, axis=1, keepdims=True) * (1.0 / OC)
        centred = jnp.where(lane < OC, conv - mean, 0.0)
        var = jnp.sum(centred * centred, axis=1, keepdims=True) * (1.0 / OC)
        scaled = centred * lax.rsqrt(var + 1e-05)
        normed = (scaled[:, 0:OC] * ngain_ref[...]).astype(BF16)
        hidden = jax.nn.gelu(
            jnp.dot(normed, up_ref[...], preferred_element_type=F32)
        ).astype(BF16)
        update = jnp.dot(hidden, down_ref[...], preferred_element_type=F32)
        mask_lane = lax.broadcasted_iota(jnp.int32, (ROWS, 128), 1)
        sea = jnp.sum(
            jnp.where(mask_lane == 64 + a, colt[0:ROWS, :], 0.0), axis=1, keepdims=True
        )
        held = drv[a + 3, :, 0:OC].astype(F32) + update
        oc_out[a] = jnp.where(sea == 1.0, held, 0.0)[0:LONS].astype(BF16)
        return carry

    lax.fori_loop(0, LATS, ocean, 0)

    def add_halves(k):
        first = CHUNKS[k][0] * CB // 128

        def step(i, carry):
            both = rspec[k][2 * i].astype(F32) + rspec[k][2 * i + 1].astype(F32)
            for t in range(CHUNKS[k][2] // 128):
                rsum[first + t, pl.ds(pl.multiple_of(i * 48, 8), 48), :] = both[
                    :, 128 * t : 128 * t + 128
                ]
            return carry

        lax.fori_loop(0, 16, step, 0)

    def z_wait(k):
        peers_all(k, z_send, z_recv, lambda copy: copy.wait_recv())

        @pl.when(self_peer)
        def _():
            z_local(k).wait()

    z_wait(1)
    add_halves(1)
    z_wait(0)
    add_halves(0)
    lane32 = lax.broadcasted_iota(jnp.int32, (32, 128), 1)

    def legendre_step(m, carry):
        planes = []
        for p in range(2):
            rows = [
                rsum[t, pl.ds(2 * m + p, 32, stride=MODES), :]
                for t in range(5)
            ]
            planes.append(rows)
        blocks = []
        for a in range(LATS):
            moves = [(p, CB * a, CB * p, CB) for p in range(2)]
            blocks.append(move_lanes(moves, 1, lambda key, t: planes[key][t], 32)[0])
        spectrum = jnp.concatenate(blocks, axis=0).astype(BF16)
        coeffs = jnp.dot(leg_p[m], spectrum, preferred_element_type=F32)
        filtered = (coeffs * sg2[...]).astype(BF16)
        synth = jnp.dot(leg_t[m], filtered, preferred_element_type=F32)
        for p in range(2):
            moves = [(a, CB * p, CB * a, CB) for a in range(LATS)]
            tiles = move_lanes(moves, 5, lambda key, t: synth[32 * key : 32 * key + 32], 32)
            for t, value in enumerate(tiles):
                ssum[t, pl.ds(2 * m + p, 32, stride=MODES), :] = value
        return carry

    lax.fori_loop(0, LATS, legendre_step, 0)

    def zi_copy(k, j):
        return pltpu.make_async_remote_copy(
            src_ref=syn[k].at[j // 2], dst_ref=rsyn[k].at[a_id], send_sem=zi_send.at[k],
            recv_sem=zi_recv.at[k], device_id=band_dev(j), device_id_type=MESH,
        )

    def zi_local(k):
        return pltpu.make_async_copy(syn[k].at[yz], rsyn[k].at[a_id], loc_sem.at[4 + k])

    def back(k):
        first = CHUNKS[k][0] * CB // 128

        def step(i, carry):
            b = lax.rem(y0 + i // 4, 4) * 4 + lax.rem(z0 + i, 4)
            for t in range(CHUNKS[k][2] // 128):
                syn[k][b, :, 128 * t : 128 * t + 128] = ssum[
                    first + t, pl.ds(pl.multiple_of(b * 48, 8), 48), :
                ].astype(BF16)
            for n in range(2):
                j = 2 * b + n
                mine = self_peer & (j == 2 * yz + h)

                @pl.when(jnp.logical_not(mine))
                def _():
                    zi_copy(k, j).start()

                @pl.when(mine)
                def _():
                    zi_local(k).start()

            return carry

        lax.fori_loop(0, 16, step, 0)

    back(0)
    back(1)

    def zi_wait(k):
        peers_all(k, zi_send, zi_recv, lambda copy: copy.wait_recv())

        @pl.when(self_peer)
        def _():
            zi_local(k).wait()

    def xi_copy(k, q):
        return pltpu.make_async_remote_copy(
            src_ref=gs[k].at[q], dst_ref=rg[k].at[me], send_sem=xi_send.at[k],
            recv_sem=xi_recv.at[k], device_id=row_dev(q), device_id_type=MESH,
        )

    def xi_local(k):
        return pltpu.make_async_copy(gs[k].at[me], rg[k].at[me], loc_sem.at[6 + k])

    def inverse(k):
        def regroup(i, carry):
            first = rsyn[k][2 * i].astype(F32)
            second = rsyn[k][2 * i + 1].astype(F32)
            for s in range(2):
                part = slice(MODES * s, MODES * s + MODES)
                both = jnp.concatenate([first[part], second[part]], axis=0)
                sy[k][s, pl.ds(pl.multiple_of(i * 48, 16), 48), :] = both.astype(BF16)
            return carry

        lax.fori_loop(0, 16, regroup, 0)

        def step(i, carry):
            xb = lax.rem(x + i, 4)
            lhs = ti[pl.ds(pl.multiple_of(xb * ROWS, 16), ROWS), :]
            for s in range(2):
                q = 2 * xb + s
                gs[k][q] = jnp.dot(lhs, sy[k][s], preferred_element_type=F32).astype(BF16)

                @pl.when(q != me)
                def _():
                    xi_copy(k, q).start()

                @pl.when(q == me)
                def _():
                    xi_local(k).start()

            return carry

        lax.fori_loop(0, 4, step, 0)

    def xi_wait(k):
        x_all(k, xi_send, xi_recv).wait_recv()
        xi_local(k).wait()

    def finish(k):
        a0, na, width = CHUNKS[k]
        for a in range(na):
            moves = [(q, CB * a, CB * q, CB) for q in range(8)]
            tiles = move_lanes(
                moves, 3,
                lambda key, t: rg[k][key, :, 128 * t : 128 * t + 128].astype(F32), ROWS,
            )
            grid = jnp.concatenate(tiles, axis=1)
            mixed = forced[a0 + a].astype(F32) + grid
            active = jax.nn.gelu(mixed).astype(BF16)
            result = mixed + jnp.dot(active, mix_ref[...], preferred_element_type=F32)
            result = result.astype(BF16)
            atm_out[a0 + a] = result[0:LONS]
            fluxes = lax.dot_general(
                fwt, result, (((1,), (1,)), ((), ())), preferred_element_type=F32
            )
            for f in range(4):
                flux_out[f, a0 + a : a0 + a + 1, :] = fluxes[f : f + 1, 0:LONS]

    ti_copy.wait()
    zi_wait(0)
    inverse(0)
    xi_wait(0)
    finish(0)
    zi_wait(1)
    inverse(1)
    xi_wait(1)
    finish(1)

    for k in range(2):
        x_all(k, x_send, x_recv).wait_send()
        x_all(k, xi_send, xi_recv).wait_send()
        peers_all(k, z_send, z_recv, lambda copy: copy.wait_send())
        peers_all(k, zi_send, zi_recv, lambda copy: copy.wait_send())
    for copy in (lat_low, lat_high, lon_low, lon_high):
        copy.wait_send()


def local(
    atmosphere, ocean_state, surface_flux, land_sea, surface_read, surface_gain, legendre,
    spectral_gain, mixing, flux_weight, flux_embed, conv_kernel, norm_gain, ocean_up, ocean_down,
):
    forward_table, inverse_table = lon_tables()
    vm = pl.BlockSpec(memory_space=pltpu.VMEM)
    hbm = pl.BlockSpec(memory_space=pl.ANY)
    wide = [w for _, _, w in CHUNKS]

    def pair(*dims):
        return [pltpu.VMEM(dims + (w,), BF16) for w in wide]

    dma = pltpu.SemaphoreType.DMA
    return pl.pallas_call(
        body,
        out_shape=(
            jax.ShapeDtypeStruct((LATS, LONS, C), BF16),
            jax.ShapeDtypeStruct((4, LATS, LONS), F32),
            jax.ShapeDtypeStruct((LATS, LONS, OC), BF16),
        ),
        in_specs=[vm] * 6 + [hbm] + [vm] * 8 + [hbm] * 2,
        out_specs=(vm, vm, vm),
        scratch_shapes=[
            pltpu.VMEM((2 * M, 4 * ROWS), BF16),
            pltpu.VMEM((4 * ROWS, 2 * M), BF16),
            pltpu.VMEM((LATS, C, C), BF16),
            pltpu.VMEM((LATS, C, C), BF16),
            pltpu.VMEM((LATS, C, C), BF16),
            pltpu.VMEM((LATS, ROWS, C), BF16),
            *pair(8, ROWS),
            *pair(2, 4, ROWS),
            *pair(PEERS, 48),
            *pair(PEERS, 48),
            pltpu.VMEM((5, 768, 128), F32),
            pltpu.VMEM((5, 768, 128), F32),
            *pair(16, 48),
            *pair(PEERS, 48),
            *pair(2, 768),
            *pair(8, ROWS),
            *pair(8, ROWS),
            pltpu.VMEM((C, 128), F32),
            pltpu.VMEM((128, 256), F32),
            pltpu.VMEM((256, 128), F32),
            pltpu.VMEM((C, 128), F32),
            pltpu.VMEM((LATS + 6, ROWS, 256), BF16),
            pltpu.VMEM((LATS + 6, 16, 256), BF16),
            pltpu.VMEM((LATS + 6, 16, 256), BF16),
            pltpu.VMEM((LATS + 6, 16, 256), BF16),
            pltpu.VMEM((LATS + 6, 16, 256), BF16),
            pltpu.VMEM((LATS + 6, ROWS, 256), F32),
            pltpu.VMEM((56, 256), F32),
            dma((3,)), dma((2,)), dma((2,)), dma((2,)), dma((2,)), dma((2,)), dma((2,)),
            dma((2,)), dma((2,)), dma((4,)), dma((4,)), dma((8,)),
        ],
        compiler_params=pltpu.CompilerParams(
            collective_id=0, has_side_effects=True, vmem_limit_bytes=VMEM_LIMIT
        ),
        name="window",
    )(
        atmosphere, ocean_state, surface_flux, land_sea, surface_read.reshape(1, OC),
        surface_gain.reshape(1, C), legendre, spectral_gain, mixing, flux_weight, flux_embed,
        conv_kernel, norm_gain.reshape(1, OC), ocean_up, ocean_down,
        jnp.asarray(forward_table), jnp.asarray(inverse_table),
    )


def solution(mesh):
    grid = P("atm", ("ocn", "ch"), None)
    return jax.shard_map(
        local,
        mesh=mesh,
        in_specs=(
            grid, grid, P(None, "atm", ("ocn", "ch")), P("atm", ("ocn", "ch")), P(), P(),
            P("atm", None, None), P(None, ("ocn", "ch")), P(), P(), P(), P(), P(), P(), P(),
        ),
        out_specs=(grid, P(None, "atm", ("ocn", "ch")), grid),
        check_vma=False,
    )
```

profile of v0, /device:TPU:1, one launch (start us, length us, event | category | flops | bytes accessed | tf_op | source)
XLA Modules:
  0.0 171.6 jit_solution(2825634909220749945)
XLA Ops:
  0.6 1.2 reshape.15.read_ref
  1.9 1.2 reshape.16.gain_ref
  3.1 1.4 copy.20.flux_ref
  4.5 1.5 copy.22.fw_ref
  6.0 1.7 copy.21.sgain_ref
  7.7 1.9 %copy.23.down_ref = bf16[800,200]{1,0:T(8,128)(2,1)} copy(bf16[800,200]{0,1:T(8,128)(2,1)} %param.31) | data formatting | bytes 640000 | tf_op args[14]
  9.6 156.6 %window.1 = (bf16[12,180,384]{2,1,0:T(8,128)(2,1)}, f32[4,12,180]{2,1,0:T(8,128)}, bf16[12,180,200]{2,1,0:T(8,128)(2,1)}) custom-call(bf16[12,180,384]{2,1,0:T(8,128)(2,1)} %atm_ref.1, bf16[12,180,200]{2,1,0:T(8,128)(2,1)} %oc_ref.1, f32[4,12,180]{2,1,0:T(8,128)} %copy.20.flux_ref, s32[12,180]{1,0:T(8,128)} %land_ref.1, bf16[1,200]{1,0:T(2,128)(2,1)} %reshape.15.read_ref, ...), custom_call_target="tpu_custom_call" | custom-call | tf_op jit(solution)/shard_map/window/pallas_call | solution.py:582
  166.2 1.5 copy.24
  167.7 0.0 copy-start
  167.7 2.9 %copy.27 = bf16[12,180,384]{2,1,0:T(8,128)(2,1)} copy(bf16[12,180,384]{2,1,0:T(8,128)(2,1)} %get-tuple-element.9) | data formatting | bytes 3317760
  170.6 0.0 copy-done
  170.6 1.0 copy.28
Async XLA Ops:
  167.7 2.9 %copy-start = (bf16[12,180,200]{2,1,0:T(8,128)(2,1)S(1)}, bf16[12,180,200]{2,1,0:T(8,128)(2,1)}, u32[]{:S(2)}) copy-start(bf16[12,180,200]{2,1,0:T(8,128)(2,1)} %get-tuple-element.11) | copy-start | bytes 2592004
where the time goes:
time: 172 us
  Pallas kernels  157 us (91%)
  local copies, waits for them, and re-layouts  14.4 us (8%)
    pallas_call x1, Pallas kernels, local(): pl.pallas_call(body, out_shape=(jax.ShapeDtypeStruct((LATS, LONS, C), BF1...  157 us
    unnamed x8, local copies, waits for them, and re-layouts  10.4 us

commit v1 on v0

--- a/solution.py
+++ b/solution.py
@@ -76,7 +76,7 @@
     tf, ti, leg, leg_p, leg_t, forced,
     pack_a, pack_b, got_a, got_b, spec_a, spec_b, rspec_a, rspec_b, rsum, ssum,
     syn_a, syn_b, rsyn_a, rsyn_b, sy_a, sy_b, gs_a, gs_b, rg_a, rg_b,
-    sg2, cols, colt, fws, drv, edge_l, edge_r, halo_l, halo_r, cpad, cker,
+    coef, filt, sgs, sg2, cols, colt, fws, drv, edge_l, edge_r, halo_l, halo_r, cpad, cker,
     in_sem, x_send, x_recv, z_send, z_recv, zi_send, zi_recv, xi_send, xi_recv, h_send, h_recv, loc_sem,
 ):
     pack, got, spec, rspec = (pack_a, pack_b), (got_a, got_b), (spec_a, spec_b), (rspec_a, rspec_b)
@@ -145,10 +145,15 @@
 
     forced[:, 176:192, :] = jnp.zeros((LATS, 16, C), BF16)
 
+    read_row = read_ref[...].astype(F32).reshape(1, OC)
+
     def force(a, carry):
-        seen = oc_ref[a].astype(F32) * read_ref[...].astype(F32)
+        seen = oc_ref[a].astype(F32) * read_row
         surface = jnp.sum(seen, axis=1, keepdims=True)
-        forced[a, 0:LONS, :] = (atm_ref[a].astype(F32) + surface * gain_ref[...]).astype(BF16)
+        for t in range(3):
+            part = slice(128 * t, 128 * t + 128)
+            total = atm_ref[a, :, part].astype(F32) + surface * gain_ref[t : t + 1, :]
+            forced[a, 0:LONS, part] = total.astype(BF16)
         return carry
 
     lax.fori_loop(0, LATS, force, 0)
@@ -203,11 +208,10 @@
     pl.semaphore_wait(barrier, 2 * n_remote + 7 + 4)
     x_start(1)
     pack_chunk(0)
-    x_start(0)
 
     cols[...] = jnp.zeros_like(cols)
-    for f in range(4):
-        cols[16 * f : 16 * f + LATS, 0:LONS] = flux_ref[f]
+    for a in range(LATS):
+        cols[4 * a : 4 * a + 4, 0:LONS] = flux_ref[a]
     cols[64 : 64 + LATS, 0:LONS] = land_ref[...].astype(F32)
     colt[...] = jnp.transpose(cols[...], (1, 0))
     drv[3:15, 176:192, :] = jnp.zeros((LATS, 16, 256), BF16)
@@ -215,7 +219,7 @@
     for a in range(LATS):
         total = oc_ref[a].astype(F32)
         for f in range(4):
-            total = total + colt[0:LONS, 16 * f + a : 16 * f + a + 1] * embed_ref[f : f + 1, :]
+            total = total + colt[0:LONS, 4 * a + f : 4 * a + f + 1] * embed_ref[f : f + 1, :]
         drv[a + 3, 0:LONS, 0:OC] = total.astype(BF16)
 
     lat_low = pltpu.make_async_remote_copy(
@@ -229,12 +233,13 @@
     lat_low.start()
     lat_high.start()
 
-    sg2[...] = jnp.zeros_like(sg2)
-    sg2[:, 0:CB] = sgain_ref[...]
-    sg2[...] = sg2[...] + pltpu.roll(sg2[...], CB, axis=1)
+    sgs[...] = jnp.zeros_like(sgs)
+    sgs[0:CB] = sgain_ref[...]
+    sgs[CB : 2 * CB] = sgain_ref[...]
+    sg2[...] = jnp.transpose(sgs[...], (1, 0))
     fws[...] = jnp.zeros_like(fws)
-    fws[:, 0:4] = fw_ref[...].astype(F32)
-    fwt = jnp.transpose(fws[...], (1, 0))[0:16].astype(BF16)
+    fws[0:4] = fw_ref[...].astype(F32)
+    fwt = fws[...].astype(BF16)
     cker[...] = jnp.zeros_like(cker)
     for i in range(7):
         cker[8 * i : 8 * i + 7, 0:OC] = ck_ref[i]
@@ -267,6 +272,12 @@
     def z_local(k):
         return pltpu.make_async_copy(spec[k].at[a_id], rspec[k].at[slot], loc_sem.at[2 + k])
 
+    lane24 = lax.broadcasted_iota(jnp.int32, (MODES, 128), 1)
+    blank = jnp.zeros((8, 128), F32)
+
+    def share(low, high):
+        return jnp.where(lane24 < 64, low, pltpu.roll(high, 64, axis=1))
+
     def forward(k):
         width = CHUNKS[k][2]
 
@@ -279,7 +290,12 @@
             ]
             for n in range(8):
                 part = slice(MODES * n, MODES * n + MODES)
-                both = jnp.concatenate([halves[0][part], halves[1][part]], axis=0)
+                low, high = halves[0][part], halves[1][part]
+                if k == 0:
+                    both = jnp.concatenate([low, high], axis=0)
+                else:
+                    tile = share(low[:, 128:256], high[:, 128:256])
+                    both = jnp.concatenate([low[:, 0:128], high[:, 0:128], tile, blank], axis=0)
                 spec[k][yb * 8 + n] = both.astype(BF16)
 
             def send(n, c2):
@@ -312,6 +328,7 @@
 
     tf_copy.wait()
     x_wait(1)
+    x_start(0)
     forward(1)
 
     lat_low.wait_recv()
@@ -377,7 +394,9 @@
         hidden = jax.nn.gelu(
             jnp.dot(normed, up_ref[...], preferred_element_type=F32)
         ).astype(BF16)
-        update = jnp.dot(hidden, down_ref[...], preferred_element_type=F32)
+        update = lax.dot_general(
+            hidden, down_ref[...], (((1,), (1,)), ((), ())), preferred_element_type=F32
+        )
         mask_lane = lax.broadcasted_iota(jnp.int32, (ROWS, 128), 1)
         sea = jnp.sum(
             jnp.where(mask_lane == 64 + a, colt[0:ROWS, :], 0.0), axis=1, keepdims=True
@@ -389,14 +408,17 @@
     lax.fori_loop(0, LATS, ocean, 0)
 
     def add_halves(k):
-        first = CHUNKS[k][0] * CB // 128
 
         def step(i, carry):
             both = rspec[k][2 * i].astype(F32) + rspec[k][2 * i + 1].astype(F32)
-            for t in range(CHUNKS[k][2] // 128):
-                rsum[first + t, pl.ds(pl.multiple_of(i * 48, 8), 48), :] = both[
-                    :, 128 * t : 128 * t + 128
-                ]
+            at = pl.ds(pl.multiple_of(i * 48, 8), 48)
+            if k == 0:
+                for t in range(3):
+                    rsum[t, at, :] = both[:, 128 * t : 128 * t + 128]
+            else:
+                rsum[3, at, :] = both[0:48]
+                tile = both[48:72]
+                rsum[4, at, :] = jnp.concatenate([tile, pltpu.roll(tile, 64, axis=1)], axis=0)
             return carry
 
         lax.fori_loop(0, 16, step, 0)
@@ -408,36 +430,57 @@
         def _():
             z_local(k).wait()
 
+    spans = ((range(0, 8), 0, 3), (range(8, LATS), 3, 5))
+
+    def gather(k, m):
+        bands, first, end = spans[k]
+        rows = {
+            (p, t): rsum[t, pl.ds(2 * m + p, 32, stride=MODES), :]
+            for p in range(2)
+            for t in range(first, end)
+        }
+        blocks = []
+        for a in bands:
+            moves = [(p, CB * a, CB * p, CB) for p in range(2)]
+            blocks.append(move_lanes(moves, 1, lambda key, t: rows[key, t], 32)[0])
+        return jnp.concatenate(blocks, axis=0).astype(BF16)
+
+    def scatter(k, m, synth):
+        bands, first, end = spans[k]
+        for p in range(2):
+            moves = [(n, CB * p, CB * a - 128 * first, CB) for n, a in enumerate(bands)]
+            tiles = move_lanes(
+                moves, end - first, lambda key, t: synth[32 * key : 32 * key + 32], 32
+            )
+            for t, value in enumerate(tiles):
+                ssum[first + t, pl.ds(2 * m + p, 32, stride=MODES), :] = value
+
+    def each_mode(work):
+        def go(i, carry):
+            for n in range(3):
+                work(3 * i + n)
+            return carry
+
+        lax.fori_loop(0, LATS // 3, go, 0)
+
+    def early(m):
+        coef[m] = jnp.dot(leg_p[m, :, 256:384], gather(1, m), preferred_element_type=F32)
+
+    def middle(m):
+        coeffs = coef[m] + jnp.dot(leg_p[m, :, 0:256], gather(0, m), preferred_element_type=F32)
+        filtered = (coeffs * sg2[...]).astype(BF16)
+        filt[m] = filtered
+        scatter(0, m, jnp.dot(leg_t[m, 0:256, :], filtered, preferred_element_type=F32))
+
+    def late(m):
+        scatter(1, m, jnp.dot(leg_t[m, 256:384, :], filt[m], preferred_element_type=F32))
+
     z_wait(1)
     add_halves(1)
+    each_mode(early)
     z_wait(0)
     add_halves(0)
-    lane32 = lax.broadcasted_iota(jnp.int32, (32, 128), 1)
-
-    def legendre_step(m, carry):
-        planes = []
-        for p in range(2):
-            rows = [
-                rsum[t, pl.ds(2 * m + p, 32, stride=MODES), :]
-                for t in range(5)
-            ]
-            planes.append(rows)
-        blocks = []
-        for a in range(LATS):
-            moves = [(p, CB * a, CB * p, CB) for p in range(2)]
-            blocks.append(move_lanes(moves, 1, lambda key, t: planes[key][t], 32)[0])
-        spectrum = jnp.concatenate(blocks, axis=0).astype(BF16)
-        coeffs = jnp.dot(leg_p[m], spectrum, preferred_element_type=F32)
-        filtered = (coeffs * sg2[...]).astype(BF16)
-        synth = jnp.dot(leg_t[m], filtered, preferred_element_type=F32)
-        for p in range(2):
-            moves = [(a, CB * p, CB * a, CB) for a in range(LATS)]
-            tiles = move_lanes(moves, 5, lambda key, t: synth[32 * key : 32 * key + 32], 32)
-            for t, value in enumerate(tiles):
-                ssum[t, pl.ds(2 * m + p, 32, stride=MODES), :] = value
-        return carry
-
-    lax.fori_loop(0, LATS, legendre_step, 0)
+    each_mode(middle)
 
     def zi_copy(k, j):
         return pltpu.make_async_remote_copy(
@@ -449,14 +492,18 @@
         return pltpu.make_async_copy(syn[k].at[yz], rsyn[k].at[a_id], loc_sem.at[4 + k])
 
     def back(k):
-        first = CHUNKS[k][0] * CB // 128
 
         def step(i, carry):
             b = lax.rem(y0 + i // 4, 4) * 4 + lax.rem(z0 + i, 4)
-            for t in range(CHUNKS[k][2] // 128):
-                syn[k][b, :, 128 * t : 128 * t + 128] = ssum[
-                    first + t, pl.ds(pl.multiple_of(b * 48, 8), 48), :
-                ].astype(BF16)
+            at = pl.ds(pl.multiple_of(b * 48, 8), 48)
+            if k == 0:
+                for t in range(3):
+                    syn[k][b, :, 128 * t : 128 * t + 128] = ssum[t, at, :].astype(BF16)
+            else:
+                last = ssum[4, at, :]
+                tile = share(last[0:MODES], last[MODES:48])
+                both = jnp.concatenate([ssum[3, at, :], tile, blank], axis=0)
+                syn[k][b] = both.astype(BF16)
             for n in range(2):
                 j = 2 * b + n
                 mine = self_peer & (j == 2 * yz + h)
@@ -474,6 +521,7 @@
         lax.fori_loop(0, 16, step, 0)
 
     back(0)
+    each_mode(late)
     back(1)
 
     def zi_wait(k):
@@ -498,8 +546,16 @@
             second = rsyn[k][2 * i + 1].astype(F32)
             for s in range(2):
                 part = slice(MODES * s, MODES * s + MODES)
+                at = pl.ds(pl.multiple_of(i * 48, 16), 48)
                 both = jnp.concatenate([first[part], second[part]], axis=0)
-                sy[k][s, pl.ds(pl.multiple_of(i * 48, 16), 48), :] = both.astype(BF16)
+                if k == 0:
+                    sy[k][s, at, :] = both.astype(BF16)
+                else:
+                    sy[k][s, at, 0:128] = both.astype(BF16)
+                    both = jnp.concatenate([first[48:72], second[48:72]], axis=0)
+                    if s:
+                        both = pltpu.roll(both, 64, axis=1)
+                    sy[k][s, at, 128:256] = both.astype(BF16)
             return carry
 
         lax.fori_loop(0, 16, regroup, 0)
@@ -544,8 +600,7 @@
             fluxes = lax.dot_general(
                 fwt, result, (((1,), (1,)), ((), ())), preferred_element_type=F32
             )
-            for f in range(4):
-                flux_out[f, a0 + a : a0 + a + 1, :] = fluxes[f : f + 1, 0:LONS]
+            flux_out[a0 + a] = fluxes[0:4, 0:LONS]
 
     ti_copy.wait()
     zi_wait(0)
@@ -578,12 +633,15 @@
     def pair(*dims):
         return [pltpu.VMEM(dims + (w,), BF16) for w in wide]
 
+    def message(count):
+        return [pltpu.VMEM((count, 48, 384), BF16), pltpu.VMEM((count, 80, 128), BF16)]
+
     dma = pltpu.SemaphoreType.DMA
-    return pl.pallas_call(
+    atm_next, flux_next, ocean_next = pl.pallas_call(
         body,
         out_shape=(
             jax.ShapeDtypeStruct((LATS, LONS, C), BF16),
-            jax.ShapeDtypeStruct((4, LATS, LONS), F32),
+            jax.ShapeDtypeStruct((LATS, 4, LONS), F32),
             jax.ShapeDtypeStruct((LATS, LONS, OC), BF16),
         ),
         in_specs=[vm] * 6 + [hbm] + [vm] * 8 + [hbm] * 2,
@@ -597,19 +655,22 @@
             pltpu.VMEM((LATS, ROWS, C), BF16),
             *pair(8, ROWS),
             *pair(2, 4, ROWS),
-            *pair(PEERS, 48),
-            *pair(PEERS, 48),
+            *message(PEERS),
+            *message(PEERS),
             pltpu.VMEM((5, 768, 128), F32),
             pltpu.VMEM((5, 768, 128), F32),
-            *pair(16, 48),
-            *pair(PEERS, 48),
+            *message(16),
+            *message(PEERS),
             *pair(2, 768),
             *pair(8, ROWS),
             *pair(8, ROWS),
+            pltpu.VMEM((LATS, C, 128), F32),
+            pltpu.VMEM((LATS, C, 128), BF16),
+            pltpu.VMEM((128, C), F32),
             pltpu.VMEM((C, 128), F32),
             pltpu.VMEM((128, 256), F32),
             pltpu.VMEM((256, 128), F32),
-            pltpu.VMEM((C, 128), F32),
+            pltpu.VMEM((16, C), F32),
             pltpu.VMEM((LATS + 6, ROWS, 256), BF16),
             pltpu.VMEM((LATS + 6, 16, 256), BF16),
             pltpu.VMEM((LATS + 6, 16, 256), BF16),
@@ -625,11 +686,13 @@
         ),
         name="window",
     )(
-        atmosphere, ocean_state, surface_flux, land_sea, surface_read.reshape(1, OC),
-        surface_gain.reshape(1, C), legendre, spectral_gain, mixing, flux_weight, flux_embed,
-        conv_kernel, norm_gain.reshape(1, OC), ocean_up, ocean_down,
+        atmosphere, ocean_state,
+        jnp.transpose(surface_flux, (1, 0, 2)), land_sea, surface_read,
+        surface_gain.reshape(3, 128), legendre, spectral_gain.T, mixing, flux_weight.T, flux_embed,
+        conv_kernel, norm_gain.reshape(1, OC), ocean_up, ocean_down.T,
         jnp.asarray(forward_table), jnp.asarray(inverse_table),
     )
+    return atm_next, jnp.transpose(flux_next, (1, 0, 2)), ocean_next
 
 
 def solution(mesh):

time: 172 us -> 160 us (0.930)
  local copies, waits for them, and re-layouts: 14.4 us -> 4.52 us
  Pallas kernels: 157 us -> 155 us
    unnamed x8 -> x7, local copies, waits for them, and re-layouts: 10.4 us -> 4.52 us
    reshape x2 -> x0, local copies, waits for them, and re-layouts: 2.48 us -> none  [the longest x1 1.24 us: local(): surface_gain.reshape(1, C)]
    pallas_call x1, Pallas kernels: 157 us -> 155 us  [local(): pl.pallas_call(body, out_shape=(jax.ShapeDtypeStruct((LATS, LONS, C), BF1...]
where the time goes in v1:
time: 160 us
  Pallas kernels  155 us (97%)
  local copies, waits for them, and re-layouts  4.52 us (3%)
    pallas_call x1, Pallas kernels, local(): pl.pallas_call(body, out_shape=(jax.ShapeDtypeStruct((LATS, LONS, C), BF1...  155 us
    unnamed x7, local copies, waits for them, and re-layouts  4.52 us

profile of v1, /device:TPU:1, one launch (start us, length us, event | category | flops | bytes accessed | tf_op | source)
XLA Modules:
  0.0 159.7 jit_solution(6546075945068803396)
XLA Ops:
  0.6 154.5 %window.1 = (bf16[12,180,384]{2,1,0:T(8,128)(2,1)}, f32[12,4,180]{2,1,0:T(4,128)}, bf16[12,180,200]{2,1,0:T(8,128)(2,1)}) custom-call(bf16[12,180,384]{2,1,0:T(8,128)(2,1)} %atm_ref.1, bf16[12,180,200]{2,1,0:T(8,128)(2,1)} %oc_ref.1, f32[12,4,180]{2,1,0:T(4,128)} %bitcast.9, s32[12,180]{1,0:T(8,128)} %land_ref.1, bf16[200]{0:T(256)(128)(2,1)} %read_ref.1, ...), custom_call_target="tpu_custom_call" | custom-call | tf_op jit(solution)/shard_map/window/pallas_call | solution.py:640
  155.2 0.0 copy-start.1
  155.2 0.0 copy-start
  155.2 2.9 %copy.23 = bf16[12,180,384]{2,1,0:T(8,128)(2,1)} copy(bf16[12,180,384]{2,1,0:T(8,128)(2,1)} %get-tuple-element.12) | data formatting | bytes 3317760
  158.1 0.0 copy-done.1
  158.1 0.6 copy.24
  158.7 0.0 copy-done
  158.7 1.0 copy.25
Async XLA Ops:
  155.2 2.9 %copy-start.1 = (f32[12,4,180]{2,1,0:T(4,128)S(1)}, f32[12,4,180]{2,1,0:T(4,128)}, u32[]{:S(2)}) copy-start(f32[12,4,180]{2,1,0:T(4,128)} %get-tuple-element.7) | copy-start | bytes 103684
  155.2 3.5 %copy-start = (bf16[12,180,200]{2,1,0:T(8,128)(2,1)S(1)}, bf16[12,180,200]{2,1,0:T(8,128)(2,1)}, u32[]{:S(2)}) copy-start(bf16[12,180,200]{2,1,0:T(8,128)(2,1)} %get-tuple-element.14) | copy-start | bytes 2592004

commit v2 on v1

--- a/solution.py
+++ b/solution.py
@@ -491,20 +491,19 @@
     def zi_local(k):
         return pltpu.make_async_copy(syn[k].at[yz], rsyn[k].at[a_id], loc_sem.at[4 + k])
 
-    def back(k):
-
+    def back(k, fill, send):
         def step(i, carry):
             b = lax.rem(y0 + i // 4, 4) * 4 + lax.rem(z0 + i, 4)
             at = pl.ds(pl.multiple_of(b * 48, 8), 48)
-            if k == 0:
+            if fill and k == 0:
                 for t in range(3):
                     syn[k][b, :, 128 * t : 128 * t + 128] = ssum[t, at, :].astype(BF16)
-            else:
+            elif fill:
                 last = ssum[4, at, :]
                 tile = share(last[0:MODES], last[MODES:48])
                 both = jnp.concatenate([ssum[3, at, :], tile, blank], axis=0)
                 syn[k][b] = both.astype(BF16)
-            for n in range(2):
+            for n in range(2 if send else 0):
                 j = 2 * b + n
                 mine = self_peer & (j == 2 * yz + h)
 
@@ -520,9 +519,11 @@
 
         lax.fori_loop(0, 16, step, 0)
 
-    back(0)
+    back(0, True, True)
     each_mode(late)
-    back(1)
+    back(1, True, False)
+    peers_all(0, zi_send, zi_recv, lambda copy: copy.wait_send())
+    back(1, False, True)
 
     def zi_wait(k):
         peers_all(k, zi_send, zi_recv, lambda copy: copy.wait_recv())
@@ -605,10 +606,10 @@
     ti_copy.wait()
     zi_wait(0)
     inverse(0)
+    zi_wait(1)
+    inverse(1)
     xi_wait(0)
     finish(0)
-    zi_wait(1)
-    inverse(1)
     xi_wait(1)
     finish(1)
 
@@ -616,7 +617,7 @@
         x_all(k, x_send, x_recv).wait_send()
         x_all(k, xi_send, xi_recv).wait_send()
         peers_all(k, z_send, z_recv, lambda copy: copy.wait_send())
-        peers_all(k, zi_send, zi_recv, lambda copy: copy.wait_send())
+    peers_all(1, zi_send, zi_recv, lambda copy: copy.wait_send())
     for copy in (lat_low, lat_high, lon_low, lon_high):
         copy.wait_send()
 

time: 160 us -> 153 us (0.956)
  Pallas kernels: 155 us -> 147 us
    pallas_call x1, Pallas kernels: 155 us -> 147 us  [local(): pl.pallas_call(body, out_shape=(jax.ShapeDtypeStruct((LATS, LONS, C), BF1...]
where the time goes in v2:
time: 153 us
  Pallas kernels  147 us (96%)
  local copies, waits for them, and re-layouts  4.52 us (3%)
    pallas_call x1, Pallas kernels, local(): pl.pallas_call(body, out_shape=(jax.ShapeDtypeStruct((LATS, LONS, C), BF1...  147 us
    unnamed x7, local copies, waits for them, and re-layouts  4.52 us

profile of v2, /device:TPU:1, one launch (start us, length us, event | category | flops | bytes accessed | tf_op | source)
XLA Modules:
  0.0 152.5 jit_solution(17258701258434429757)
XLA Ops:
  0.6 147.3 %window.1 = (bf16[12,180,384]{2,1,0:T(8,128)(2,1)}, f32[12,4,180]{2,1,0:T(4,128)}, bf16[12,180,200]{2,1,0:T(8,128)(2,1)}) custom-call(bf16[12,180,384]{2,1,0:T(8,128)(2,1)} %atm_ref.1, bf16[12,180,200]{2,1,0:T(8,128)(2,1)} %oc_ref.1, f32[12,4,180]{2,1,0:T(4,128)} %bitcast.9, s32[12,180]{1,0:T(8,128)} %land_ref.1, bf16[200]{0:T(256)(128)(2,1)} %read_ref.1, ...), custom_call_target="tpu_custom_call" | custom-call | tf_op jit(solution)/shard_map/window/pallas_call | solution.py:641
  148.0 0.0 copy-start.1
  148.0 0.0 copy-start
  148.0 2.9 %copy.23 = bf16[12,180,384]{2,1,0:T(8,128)(2,1)} copy(bf16[12,180,384]{2,1,0:T(8,128)(2,1)} %get-tuple-element.12) | data formatting | bytes 3317760
  150.9 0.0 copy-done.1
  150.9 0.6 copy.24
  151.5 0.0 copy-done
  151.5 1.0 copy.25
Async XLA Ops:
  148.0 2.9 %copy-start.1 = (f32[12,4,180]{2,1,0:T(4,128)S(1)}, f32[12,4,180]{2,1,0:T(4,128)}, u32[]{:S(2)}) copy-start(f32[12,4,180]{2,1,0:T(4,128)} %get-tuple-element.7) | copy-start | bytes 103684
  148.0 3.5 %copy-start = (bf16[12,180,200]{2,1,0:T(8,128)(2,1)S(1)}, bf16[12,180,200]{2,1,0:T(8,128)(2,1)}, u32[]{:S(2)}) copy-start(bf16[12,180,200]{2,1,0:T(8,128)(2,1)} %get-tuple-element.14) | copy-start | bytes 2592004

commit v3 on v2

--- a/solution.py
+++ b/solution.py
@@ -74,7 +74,7 @@
     embed_ref, ck_ref, ngain_ref, up_ref, down_ref, tf_hbm, ti_hbm,
     atm_out, flux_out, oc_out,
     tf, ti, leg, leg_p, leg_t, forced,
-    pack_a, pack_b, got_a, got_b, spec_a, spec_b, rspec_a, rspec_b, rsum, ssum,
+    pack_a, pack_b, got_a, got_b, gin, spec_a, spec_b, rspec_a, rspec_b, rsum, ssum,
     syn_a, syn_b, rsyn_a, rsyn_b, sy_a, sy_b, gs_a, gs_b, rg_a, rg_b,
     coef, filt, sgs, sg2, cols, colt, fws, drv, edge_l, edge_r, halo_l, halo_r, cpad, cker,
     in_sem, x_send, x_recv, z_send, z_recv, zi_send, zi_recv, xi_send, xi_recv, h_send, h_recv, loc_sem,
@@ -158,23 +158,43 @@
 
     lax.fori_loop(0, LATS, force, 0)
 
+    def share(low, high):
+        lanes = lax.broadcasted_iota(jnp.int32, low.shape, 1)
+        return jnp.where(lanes < 64, low, pltpu.roll(high, 64, axis=1))
+
     def pack_chunk(k):
         a0, na, width = CHUNKS[k]
 
-        def rows_step(rb, carry):
-            r0 = pl.multiple_of(rb * 48, 16)
+        def pieces(r0):
             held = {}
             for a in range(na):
                 for t in range(3):
                     held[a, t] = forced[a0 + a, pl.ds(r0, 48), 128 * t : 128 * t + 128].astype(F32)
             for q in range(8):
                 moves = [(a, CB * q, CB * a, CB) for a in range(na)]
-                tiles = move_lanes(moves, width // 128, lambda key, t: held[key, t], 48)
+                yield q, move_lanes(moves, width // 128, lambda key, t: held[key, t], 48)
+
+        def whole_step(rb, carry):
+            r0 = pl.multiple_of(rb * 48, 16)
+            for q, tiles in pieces(r0):
                 for t, value in enumerate(tiles):
                     pack[k][q, pl.ds(r0, 48), 128 * t : 128 * t + 128] = value.astype(BF16)
             return carry
 
-        lax.fori_loop(0, 4, rows_step, 0)
+        def shared_step(rb, carry):
+            r0 = pl.multiple_of(rb * 48, 16)
+            r1 = pl.multiple_of(rb * 48 + 96, 16)
+            r2 = pl.multiple_of(rb * 48 + ROWS, 16)
+            for (q, low), (_, high) in zip(pieces(r0), pieces(r1)):
+                pack[k][q, pl.ds(r0, 48), :] = low[0].astype(BF16)
+                pack[k][q, pl.ds(r1, 48), :] = high[0].astype(BF16)
+                pack[k][q, pl.ds(r2, 48), :] = share(low[1], high[1]).astype(BF16)
+            return carry
+
+        if k == 0:
+            lax.fori_loop(0, 4, whole_step, 0)
+        else:
+            lax.fori_loop(0, 2, shared_step, 0)
 
     def x_copy(k, q):
         return pltpu.make_async_remote_copy(
@@ -244,23 +264,6 @@
     for i in range(7):
         cker[8 * i : 8 * i + 7, 0:OC] = ck_ref[i]
 
-    leg_copy.wait()
-    new = lax.broadcasted_iota(jnp.int32, (C, C), 0)
-    old = lax.broadcasted_iota(jnp.int32, (C, C), 1)
-    order = (old == lax.rem(new, 32) * LATS + new // 32).astype(F32).astype(BF16)
-
-    def permute(m, carry):
-        table = leg[m]
-        leg_p[m] = lax.dot_general(
-            table, order, (((1,), (1,)), ((), ())), preferred_element_type=F32
-        ).astype(BF16)
-        leg_t[m] = lax.dot_general(
-            order, table, (((1,), (1,)), ((), ())), preferred_element_type=F32
-        ).astype(BF16)
-        return carry
-
-    lax.fori_loop(0, LATS, permute, 0)
-
     slot = 2 * yz + h
 
     def z_copy(k, j):
@@ -272,20 +275,27 @@
     def z_local(k):
         return pltpu.make_async_copy(spec[k].at[a_id], rspec[k].at[slot], loc_sem.at[2 + k])
 
-    lane24 = lax.broadcasted_iota(jnp.int32, (MODES, 128), 1)
     blank = jnp.zeros((8, 128), F32)
-
-    def share(low, high):
-        return jnp.where(lane24 < 64, low, pltpu.roll(high, 64, axis=1))
 
     def forward(k):
         width = CHUNKS[k][2]
+        if k == 1:
+            for s in range(2):
+                for n in range(4):
+                    gin[s, ROWS * n : ROWS * n + ROWS, 0:128] = got[k][s, n, 0:ROWS, :]
+                    tile = got[k][s, n, ROWS:288, :]
+                    gin[s, ROWS * n : ROWS * n + 96, 128:256] = tile
+                    turned = pltpu.roll(tile.astype(F32), 64, axis=1).astype(BF16)
+                    gin[s, ROWS * n + 96 : ROWS * n + ROWS, 128:256] = turned
+
+        def rhs(s):
+            return gin[s] if k == 1 else got[k][s].reshape(4 * ROWS, width)
 
         def step(i, carry):
             yb = lax.rem(y0 + i, 4)
             lhs = tf[pl.ds(pl.multiple_of(yb * 192, 16), 192), :]
             halves = [
-                jnp.dot(lhs, got[k][s].reshape(4 * ROWS, width), preferred_element_type=F32)
+                jnp.dot(lhs, rhs(s), preferred_element_type=F32)
                 for s in range(2)
             ]
             for n in range(8):
@@ -354,6 +364,23 @@
     )
     lon_low.start()
     lon_high.start()
+
+    leg_copy.wait()
+    new = lax.broadcasted_iota(jnp.int32, (C, C), 0)
+    old = lax.broadcasted_iota(jnp.int32, (C, C), 1)
+    order = (old == lax.rem(new, 32) * LATS + new // 32).astype(F32).astype(BF16)
+
+    def permute(m, carry):
+        table = leg[m]
+        leg_p[m] = lax.dot_general(
+            table, order, (((1,), (1,)), ((), ())), preferred_element_type=F32
+        ).astype(BF16)
+        leg_t[m] = lax.dot_general(
+            order, table, (((1,), (1,)), ((), ())), preferred_element_type=F32
+        ).astype(BF16)
+        return carry
+
+    lax.fori_loop(0, LATS, permute, 0)
 
     x_wait(0)
     forward(0)
@@ -566,7 +593,11 @@
             lhs = ti[pl.ds(pl.multiple_of(xb * ROWS, 16), ROWS), :]
             for s in range(2):
                 q = 2 * xb + s
-                gs[k][q] = jnp.dot(lhs, sy[k][s], preferred_element_type=F32).astype(BF16)
+                values = jnp.dot(lhs, sy[k][s], preferred_element_type=F32)
+                if k == 1:
+                    tile = share(values[0:96, 128:256], values[96:ROWS, 128:256])
+                    values = jnp.concatenate([values[:, 0:128], tile], axis=0)
+                gs[k][q] = values.astype(BF16)
 
                 @pl.when(q != me)
                 def _():
@@ -586,12 +617,18 @@
 
     def finish(k):
         a0, na, width = CHUNKS[k]
+
+        def came(q, t):
+            if k == 0:
+                return rg[k][q, :, 128 * t : 128 * t + 128].astype(F32)
+            if t == 0:
+                return rg[k][q, 0:ROWS, :].astype(F32)
+            tile = rg[k][q, ROWS:288, :].astype(F32)
+            return jnp.concatenate([tile, pltpu.roll(tile, 64, axis=1)], axis=0)
+
         for a in range(na):
             moves = [(q, CB * a, CB * q, CB) for q in range(8)]
-            tiles = move_lanes(
-                moves, 3,
-                lambda key, t: rg[k][key, :, 128 * t : 128 * t + 128].astype(F32), ROWS,
-            )
+            tiles = move_lanes(moves, 3, came, ROWS)
             grid = jnp.concatenate(tiles, axis=1)
             mixed = forced[a0 + a].astype(F32) + grid
             active = jax.nn.gelu(mixed).astype(BF16)
@@ -636,6 +673,9 @@
 
     def message(count):
         return [pltpu.VMEM((count, 48, 384), BF16), pltpu.VMEM((count, 80, 128), BF16)]
+
+    def crossing(*dims):
+        return [pltpu.VMEM(dims + (ROWS, 384), BF16), pltpu.VMEM(dims + (288, 128), BF16)]
 
     dma = pltpu.SemaphoreType.DMA
     atm_next, flux_next, ocean_next = pl.pallas_call(
@@ -654,8 +694,9 @@
             pltpu.VMEM((LATS, C, C), BF16),
             pltpu.VMEM((LATS, C, C), BF16),
             pltpu.VMEM((LATS, ROWS, C), BF16),
-            *pair(8, ROWS),
-            *pair(2, 4, ROWS),
+            *crossing(8),
+            *crossing(2, 4),
+            pltpu.VMEM((2, 4 * ROWS, 256), BF16),
             *message(PEERS),
             *message(PEERS),
             pltpu.VMEM((5, 768, 128), F32),
@@ -663,8 +704,8 @@
             *message(16),
             *message(PEERS),
             *pair(2, 768),
-            *pair(8, ROWS),
-            *pair(8, ROWS),
+            *crossing(8),
+            *crossing(8),
             pltpu.VMEM((LATS, C, 128), F32),
             pltpu.VMEM((LATS, C, 128), BF16),
             pltpu.VMEM((128, C), F32),

time: 153 us -> 149 us (0.974)
  Pallas kernels: 147 us -> 144 us
    pallas_call x1, Pallas kernels: 147 us -> 144 us  [local(): pl.pallas_call(body, out_shape=(jax.ShapeDtypeStruct((LATS, LONS, C), BF1...]
where the time goes in v3:
time: 149 us
  Pallas kernels  144 us (97%)
  local copies, waits for them, and re-layouts  4.52 us (3%)
    pallas_call x1, Pallas kernels, local(): pl.pallas_call(body, out_shape=(jax.ShapeDtypeStruct((LATS, LONS, C), BF1...  144 us
    unnamed x7, local copies, waits for them, and re-layouts  4.52 us

profile of v3, /device:TPU:1, one launch (start us, length us, event | category | flops | bytes accessed | tf_op | source)
XLA Modules:
  0.0 148.8 jit_solution(8047197657431805241)
XLA Ops:
  0.6 143.6 %window.1 = (bf16[12,180,384]{2,1,0:T(8,128)(2,1)}, f32[12,4,180]{2,1,0:T(4,128)}, bf16[12,180,200]{2,1,0:T(8,128)(2,1)}) custom-call(bf16[12,180,384]{2,1,0:T(8,128)(2,1)} %atm_ref.1, bf16[12,180,200]{2,1,0:T(8,128)(2,1)} %oc_ref.1, f32[12,4,180]{2,1,0:T(4,128)} %bitcast.9, s32[12,180]{1,0:T(8,128)} %land_ref.1, bf16[200]{0:T(256)(128)(2,1)} %read_ref.1, ...), custom_call_target="tpu_custom_call" | custom-call | tf_op jit(solution)/shard_map/window/pallas_call | solution.py:681
  144.3 0.0 copy-start.1
  144.3 0.0 copy-start
  144.3 2.9 %copy.23 = bf16[12,180,384]{2,1,0:T(8,128)(2,1)} copy(bf16[12,180,384]{2,1,0:T(8,128)(2,1)} %get-tuple-element.12) | data formatting | bytes 3317760
  147.2 0.0 copy-done.1
  147.2 0.6 copy.24
  147.8 0.0 copy-done
  147.8 1.0 copy.25
Async XLA Ops:
  144.3 2.9 %copy-start.1 = (f32[12,4,180]{2,1,0:T(4,128)S(1)}, f32[12,4,180]{2,1,0:T(4,128)}, u32[]{:S(2)}) copy-start(f32[12,4,180]{2,1,0:T(4,128)} %get-tuple-element.7) | copy-start | bytes 103684
  144.3 3.5 %copy-start = (bf16[12,180,200]{2,1,0:T(8,128)(2,1)S(1)}, bf16[12,180,200]{2,1,0:T(8,128)(2,1)}, u32[]{:S(2)}) copy-start(bf16[12,180,200]{2,1,0:T(8,128)(2,1)} %get-tuple-element.14) | copy-start | bytes 2592004

commit v4 on v3

--- a/solution.py
+++ b/solution.py
@@ -156,7 +156,7 @@
             forced[a, 0:LONS, part] = total.astype(BF16)
         return carry
 
-    lax.fori_loop(0, LATS, force, 0)
+    lax.fori_loop(CHUNKS[1][0], LATS, force, 0)
 
     def share(low, high):
         lanes = lax.broadcasted_iota(jnp.int32, low.shape, 1)
@@ -227,6 +227,7 @@
     pack_chunk(1)
     pl.semaphore_wait(barrier, 2 * n_remote + 7 + 4)
     x_start(1)
+    lax.fori_loop(0, CHUNKS[1][0], force, 0)
     pack_chunk(0)
 
     cols[...] = jnp.zeros_like(cols)

time: 149 us -> 150 us (level)
  no operation moved by 1% of the time
where the time goes in v4:
time: 150 us; the launch traced here: 149 us
  Pallas kernels  144 us (96%)
  local copies, waits for them, and re-layouts  4.52 us (3%)
    pallas_call x1, Pallas kernels, local(): pl.pallas_call(body, out_shape=(jax.ShapeDtypeStruct((LATS, LONS, C), BF1...  144 us
    unnamed x7, local copies, waits for them, and re-layouts  4.52 us

profile of v4, /device:TPU:1, one launch (start us, length us, event | category | flops | bytes accessed | tf_op | source)
XLA Modules:
  0.0 149.3 jit_solution(13050832691852674592)
XLA Ops:
  0.6 144.1 %window.1 = (bf16[12,180,384]{2,1,0:T(8,128)(2,1)}, f32[12,4,180]{2,1,0:T(4,128)}, bf16[12,180,200]{2,1,0:T(8,128)(2,1)}) custom-call(bf16[12,180,384]{2,1,0:T(8,128)(2,1)} %atm_ref.1, bf16[12,180,200]{2,1,0:T(8,128)(2,1)} %oc_ref.1, f32[12,4,180]{2,1,0:T(4,128)} %bitcast.9, s32[12,180]{1,0:T(8,128)} %land_ref.1, bf16[200]{0:T(256)(128)(2,1)} %read_ref.1, ...), custom_call_target="tpu_custom_call" | custom-call | tf_op jit(solution)/shard_map/window/pallas_call | solution.py:682
  144.8 0.0 copy-start.1
  144.8 0.0 copy-start
  144.8 2.9 %copy.23 = bf16[12,180,384]{2,1,0:T(8,128)(2,1)} copy(bf16[12,180,384]{2,1,0:T(8,128)(2,1)} %get-tuple-element.12) | data formatting | bytes 3317760
  147.7 0.0 copy-done.1
  147.7 0.6 copy.24
  148.3 0.0 copy-done
  148.3 1.0 copy.25
Async XLA Ops:
  144.8 2.9 %copy-start.1 = (f32[12,4,180]{2,1,0:T(4,128)S(1)}, f32[12,4,180]{2,1,0:T(4,128)}, u32[]{:S(2)}) copy-start(f32[12,4,180]{2,1,0:T(4,128)} %get-tuple-element.7) | copy-start | bytes 103684
  144.8 3.5 %copy-start = (bf16[12,180,200]{2,1,0:T(8,128)(2,1)S(1)}, bf16[12,180,200]{2,1,0:T(8,128)(2,1)}, u32[]{:S(2)}) copy-start(bf16[12,180,200]{2,1,0:T(8,128)(2,1)} %get-tuple-element.14) | copy-start | bytes 2592004

commit v5 on v3

--- a/solution.py
+++ b/solution.py
@@ -337,8 +337,9 @@
             act(covers(rspec[k], send.at[k], recv.at[k]))
 
     tf_copy.wait()
+    x_all(1, x_send, x_recv).wait_send()
+    x_start(0)
     x_wait(1)
-    x_start(0)
     forward(1)
 
     lat_low.wait_recv()
@@ -650,8 +651,8 @@
     xi_wait(1)
     finish(1)
 
+    x_all(0, x_send, x_recv).wait_send()
     for k in range(2):
-        x_all(k, x_send, x_recv).wait_send()
         x_all(k, xi_send, xi_recv).wait_send()
         peers_all(k, z_send, z_recv, lambda copy: copy.wait_send())
     peers_all(1, zi_send, zi_recv, lambda copy: copy.wait_send())

time: 149 us -> 150 us (level)
  no operation moved by 1% of the time
where the time goes in v5:
time: 150 us; the launch traced here: 149 us
  Pallas kernels  144 us (96%)
  local copies, waits for them, and re-layouts  4.52 us (3%)
    pallas_call x1, Pallas kernels, local(): pl.pallas_call(body, out_shape=(jax.ShapeDtypeStruct((LATS, LONS, C), BF1...  144 us
    unnamed x7, local copies, waits for them, and re-layouts  4.52 us

profile of v5, /device:TPU:1, one launch (start us, length us, event | category | flops | bytes accessed | tf_op | source)
XLA Modules:
  0.0 149.4 jit_solution(4104722590062080672)
XLA Ops:
  0.6 144.2 %window.1 = (bf16[12,180,384]{2,1,0:T(8,128)(2,1)}, f32[12,4,180]{2,1,0:T(4,128)}, bf16[12,180,200]{2,1,0:T(8,128)(2,1)}) custom-call(bf16[12,180,384]{2,1,0:T(8,128)(2,1)} %atm_ref.1, bf16[12,180,200]{2,1,0:T(8,128)(2,1)} %oc_ref.1, f32[12,4,180]{2,1,0:T(4,128)} %bitcast.9, s32[12,180]{1,0:T(8,128)} %land_ref.1, bf16[200]{0:T(256)(128)(2,1)} %read_ref.1, ...), custom_call_target="tpu_custom_call" | custom-call | tf_op jit(solution)/shard_map/window/pallas_call | solution.py:682
  144.9 0.0 copy-start.1
  144.9 0.0 copy-start
  144.9 2.9 %copy.23 = bf16[12,180,384]{2,1,0:T(8,128)(2,1)} copy(bf16[12,180,384]{2,1,0:T(8,128)(2,1)} %get-tuple-element.12) | data formatting | bytes 3317760
  147.8 0.0 copy-done.1
  147.8 0.6 copy.24
  148.4 0.0 copy-done
  148.4 1.0 copy.25
Async XLA Ops:
  144.9 2.9 %copy-start.1 = (f32[12,4,180]{2,1,0:T(4,128)S(1)}, f32[12,4,180]{2,1,0:T(4,128)}, u32[]{:S(2)}) copy-start(f32[12,4,180]{2,1,0:T(4,128)} %get-tuple-element.7) | copy-start | bytes 103684
  144.9 3.5 %copy-start = (bf16[12,180,200]{2,1,0:T(8,128)(2,1)S(1)}, bf16[12,180,200]{2,1,0:T(8,128)(2,1)}, u32[]{:S(2)}) copy-start(bf16[12,180,200]{2,1,0:T(8,128)(2,1)} %get-tuple-element.14) | copy-start | bytes 2592004
